TPU v7x, 32 devices: a whole 2x2x4 slice. The times are simulated.
32 devices in a mesh: ctx: 8 (over y, x, core), vocab: 4 (over z).
Axes of the slice: x: 2, y: 2, z: 4, core: 2. Of those that a mesh axis runs over, the one named last changes fastest.
Arguments:
- block_query: bfloat16 [256, 6144], P('ctx', 'vocab'), may hold values from -16 to 16
- block_key: bfloat16 [256, 6144], P('ctx', 'vocab'), may hold values from -16 to 16
- block_value: bfloat16 [256, 6144], P('ctx', 'vocab'), may hold values from -6 to 6
- block_doc: int32 [256], P('ctx'), may hold values from 0 to 1, never falling along the last dimension, each value on 1 to 224 neighbouring positions
- token_query: bfloat16 [1024, 6144], P(('ctx', 'vocab')), may hold values from -16 to 16
- token_key: bfloat16 [1024, 6144], P(('ctx', 'vocab')), may hold values from -16 to 16
- token_value: bfloat16 [1024, 6144], P(('ctx', 'vocab')), may hold values from -600 to 600
- token_state: bfloat16 [1024, 6144], P(('ctx', 'vocab')), may hold values from -6 to 6
- norm_gain: float32 [6144], replicated, may hold values from 0.5 to 1.5
- head_weight: bfloat16 [6144, 32768], P(None, ('ctx', 'vocab')), may hold values from -128 to 128
- targets: int32 [1024], replicated, may hold values from 0 to 32767
Outputs:
- block_context: bfloat16 [256, 6144], P('ctx', 'vocab')
- token_prior: float32 [1024], P(('ctx', 'vocab'))
Inputs may be any that keep to these rules, and one draw needn't show every extreme that they name: block_doc never falls along the blocks; no document holds more than 224 blocks.
All inputs are finite; a program needn't handle non-finite values.
Results may differ from a plain program's by a relative error of at most 0.005.
Values may be sent and summed in bfloat16 or wider, within the bound.
A program may use at most 128 MiB of HBM per device.

v0:
```python
import math

import jax
import jax.numpy as jnp
from jax import lax
from jax.sharding import PartitionSpec as P

HEAD_DIM = 128
BLOCK_LEN = 4


big_negative = -1e30


def local_decoder(context, token_query, token_key, token_value, token_state, norm_gain):
    scale = 1.0 / math.sqrt(HEAD_DIM)
    groups = context.shape[0]
    width = context.shape[1]
    head_total = width // HEAD_DIM
    shape = (groups, BLOCK_LEN, head_total, HEAD_DIM)
    prefix = context.reshape(groups, 1, head_total, HEAD_DIM)
    queries = token_query.reshape(shape)
    keys = jnp.concatenate([prefix, token_key.reshape(shape)], axis=1)
    values = jnp.concatenate([prefix, token_value.reshape(shape)], axis=1)
    scores = (
        jnp.einsum("bihd,bjhd->bhij", queries, keys, preferred_element_type=jnp.float32) * scale
    )
    allowed = (
        jnp.arange(BLOCK_LEN + 1, dtype=jnp.int32)[None, :]
        <= jnp.arange(BLOCK_LEN, dtype=jnp.int32)[:, None] + 1
    )
    scores = jnp.where(allowed, scores, -jnp.inf)
    highest = jnp.max(scores, axis=-1, keepdims=True)
    weights = jnp.exp(scores - highest)
    totals = jnp.sum(weights, axis=-1)
    mixed = jnp.einsum(
        "bhij,bjhd->bihd", weights.astype(jnp.bfloat16), values, preferred_element_type=jnp.float32
    )
    mixed = mixed / jnp.transpose(totals, (0, 2, 1))[..., None]
    summed = token_state.astype(jnp.float32) + mixed.reshape(groups * BLOCK_LEN, width)
    power = jnp.mean(summed * summed, axis=-1, keepdims=True)
    return (summed * lax.rsqrt(power + 1e-05) * norm_gain).astype(jnp.bfloat16)


def local(
    block_query,
    block_key,
    block_value,
    block_doc,
    token_query,
    token_key,
    token_value,
    token_state,
    norm_gain,
    head_weight,
    targets,
):
    local_rows = block_query.shape[0]
    head_count = block_query.shape[1] // HEAD_DIM
    scale = 1.0 / math.sqrt(HEAD_DIM)
    first_row = lax.axis_index("ctx") * local_rows
    queries = block_query.reshape(local_rows, head_count, HEAD_DIM)
    own_doc = block_doc.astype(jnp.bfloat16)
    query_places = first_row + jnp.arange(local_rows, dtype=jnp.int32)
    highest = jnp.full((local_rows, head_count), big_negative, jnp.float32)
    keys = lax.all_gather(block_key, "ctx", axis=0, tiled=True)
    values = lax.all_gather(block_value, "ctx", axis=0, tiled=True)
    docs = lax.all_gather(own_doc, "ctx", axis=0, tiled=True)
    count = keys.shape[0]
    keys = keys.reshape(count, head_count, HEAD_DIM)
    values = values.reshape(count, head_count, HEAD_DIM)
    scores = jnp.einsum("qhd,khd->qhk", queries, keys, preferred_element_type=jnp.float32) * scale
    key_places = jnp.arange(count, dtype=jnp.int32)
    allowed = (query_places[:, None] >= key_places[None, :]) & (own_doc[:, None] == docs[None, :])
    allowed = allowed[:, None, :]
    newest = jnp.maximum(highest, jnp.max(jnp.where(allowed, scores, big_negative), axis=-1))
    weights = jnp.where(allowed, jnp.exp(scores - newest[..., None]), 0.0)
    totals = jnp.sum(weights, axis=-1)
    update = jnp.einsum(
        "qhk,khd->qhd", weights.astype(jnp.bfloat16), values, preferred_element_type=jnp.float32
    )
    mixed = update
    highest, totals, mixed = (newest, totals, mixed)
    block_context = (
        (mixed / totals[..., None]).reshape(local_rows, head_count * HEAD_DIM).astype(jnp.bfloat16)
    )
    grouped = lax.all_to_all(block_context, "vocab", split_axis=0, concat_axis=1, tiled=True)
    hidden = local_decoder(grouped, token_query, token_key, token_value, token_state, norm_gain)
    vocab_cols = head_weight.shape[1]
    col_start = lax.axis_index(("ctx", "vocab")) * vocab_cols
    columns = jnp.arange(vocab_cols, dtype=jnp.int32)
    piece = lax.all_gather(hidden, ("ctx", "vocab"), axis=0, tiled=True)
    logits = jnp.dot(piece, head_weight, preferred_element_type=jnp.float32)
    top = jnp.max(logits, axis=-1)
    mass = jnp.sum(jnp.exp(logits - top[:, None]), axis=-1)
    wanted = targets - col_start
    picked = jnp.sum(jnp.where(columns[None, :] == wanted[:, None], logits, 0.0), axis=1)
    peaks = top
    masses = mass
    picks = picked
    stats = (peaks, masses, picks)
    peaks = lax.pmax(stats[0], ("ctx", "vocab"))
    masses, picks = lax.psum((stats[1] * jnp.exp(stats[0] - peaks), stats[2]), ("ctx", "vocab"))
    priors = picks - (peaks + jnp.log(masses))
    own_count = hidden.shape[0]
    token_prior = lax.dynamic_slice_in_dim(
        priors, lax.axis_index(("ctx", "vocab")) * own_count, own_count
    )
    return (block_context, token_prior)


def solution(mesh):
    placed = (
        P("ctx", "vocab"),
        P("ctx", "vocab"),
        P("ctx", "vocab"),
        P("ctx"),
        P(("ctx", "vocab"), None),
        P(("ctx", "vocab"), None),
        P(("ctx", "vocab"), None),
        P(("ctx", "vocab"), None),
        P(),
        P(None, ("ctx", "vocab")),
        P(),
    )
    return jax.shard_map(
        local,
        mesh=mesh,
        in_specs=placed,
        out_specs=(P("ctx", "vocab"), P(("ctx", "vocab"))),
        check_vma=False,
    )
```

profile of v0, /device:TPU:0, one launch (start us, length us, event | category | flops | bytes accessed | tf_op | source)
XLA Modules:
  0.0 266.6 jit_solution(1872366244450607800)
XLA Ops:
  7.2 0.7 convert_element_type.25
  7.9 1.2 dynamic-slice
  9.8 0.2 dynamic-update-slice
  10.0 15.1 %all-reduce = bf16[256]{0:T(256)(128)(2,1)S(1)} all-reduce(bf16[256]{0:T(256)(128)(2,1)S(1)} %dynamic-update-slice), channel_id=1, replica_groups=mesh['ctx'=8,'vocab'=4] {'ctx'}, use_global_device_ids=true, to_apply=%add | all-reduce | flops 256 | bytes 1024
  25.1 9.8 %all_gather.13 = bf16[256,1536]{1,0:T(8,128)(2,1)S(1)} all-gather(bf16[32,1536]{1,0:T(8,128)(2,1)} %param.12), channel_id=1, replica_groups=mesh['ctx'=8,'vocab'=4] {'ctx'}, dimensions={0}, use_global_device_ids=true | all-gather | bytes 884736 | tf_op jit(solution)/shard_map/all_gather | solution.py:66
  34.9 0.3 copy.29
  35.2 0.1 fusion.21
  35.3 0.3 select_reduce_fusion.1
  35.6 10.1 %all_gather.14 = bf16[256,1536]{1,0:T(8,128)(2,1)S(1)} all-gather(bf16[32,1536]{1,0:T(8,128)(2,1)} %param.13), channel_id=1, replica_groups=mesh['ctx'=8,'vocab'=4] {'ctx'}, dimensions={0}, use_global_device_ids=true | all-gather | bytes 884736 | tf_op jit(solution)/shard_map/all_gather | solution.py:67
  45.7 0.3 copy.32
  46.0 0.2 fusion.13
  46.2 0.4 fusion.5
  46.7 0.7 convert_element_type.30
  47.4 4.9 %all-to-all-start = ((bf16[4,8,1536]{2,1,0:T(8,128)(2,1)}), bf16[4,8,1536]{2,1,0:T(8,128)(2,1)S(1)}, u32[]{:S(2)}, u32[]{:S(2)}) async-start(bf16[4,8,1536]{2,1,0:T(8,128)(2,1)} %convert_element_type.30), calls=%async_computation | async-start | bytes 196608 | tf_op jit(solution)/shard_map/all_to_all | solution.py:87
  52.3 0.1 copy.48
  52.4 0.2 copy.40
  52.7 0.2 copy.38
  52.8 0.1 iota_compare_fusion.2
  52.9 5.4 %all-to-all-done = bf16[4,8,1536]{2,1,0:T(8,128)(2,1)S(1)} async-done(((bf16[4,8,1536]{2,1,0:T(8,128)(2,1)}), bf16[4,8,1536]{2,1,0:T(8,128)(2,1)S(1)}, u32[]{:S(2)}, u32[]{:S(2)}) %all-to-all-start) | async-done | bytes 98336 | tf_op jit(solution)/shard_map/all_to_all | solution.py:87
  58.4 0.9 fusion.25
  59.3 0.9 fusion.8
  60.2 1.2 fusion.2
  61.5 0.1 copy.42
  61.6 0.4 multiply_reduce_fusion
  61.9 1.0 multiply_convert_fusion
  63.0 0.6 copy_bitcast_fusion
  63.7 93.5 %all-gather.2.cloned.1.call-done = bf16[1024,6144]{1,0:T(8,128)(2,1)} async-done(((bf16[32,6144]{1,0:T(8,128)(2,1)}), bf16[1024,6144]{1,0:T(8,128)(2,1)}) %all-gather.2.cloned.1.call-update) | async-done | bytes 12582928 | tf_op jit(solution)/shard_map/all_gather | solution.py:92
  157.2 19.4 %fusion.26 = (f32[1024]{0:T(1024)S(1)}, f32[1024,1024]{0,1:T(8,128)}) fusion(bf16[1024,6144]{1,0:T(8,128)(2,1)} %all-gather.2.cloned.1.call-done, bf16[6144,1024]{1,0:T(8,128)(2,1)} %param.20), kind=kOutput, calls=%fused_computation.49 | convolution fusion | flops 12885949440 | bytes 29364224 | tf_op jit(solution)/shard_map/dot_general | solution.py:93
  176.6 38.6 %pmax.7 = f32[1024]{0:T(1024)S(1)} all-reduce(f32[1024]{0:T(1024)S(1)} %get-tuple-element.10), channel_id=1, replica_groups=mesh['ctx'=8,'vocab'=4] {'ctx','vocab'}, use_global_device_ids=true, to_apply=%region_8.9 | all-reduce | flops 1024 | bytes 8192 | tf_op jit(solution)/shard_map/pmax | solution.py:102
  215.1 3.3 %exponential_reduce_fusion = (f32[1024]{0:T(1024)S(1)}, f32[1024]{0:T(1024)S(1)}) fusion(f32[1024,1024]{0,1:T(8,128)} %get-tuple-element.11, f32[1024]{0:T(1024)S(1)} %get-tuple-element.10, s32[1024]{0:T(1024)S(1)} %broadcast_subtract_fusion), kind=kLoop, calls=%fused_computation | loop fusion | flops 5240832 | bytes 4210688 | tf_op jit(solution)/shard_map/reduce_sum | solution.py:95
  218.5 40.7 %all-reduce.1 = (f32[1024]{0:T(1024)S(1)}, f32[1024]{0:T(1024)S(1)}) all-reduce(f32[1024]{0:T(1024)S(1)} %get-tuple-element.3, f32[1024]{0:T(1024)S(1)} %exponential_multiply_fusion), channel_id=1, replica_groups=mesh['ctx'=8,'vocab'=4] {'ctx','vocab'}, use_global_device_ids=true, to_apply=%region_6.7 | all-reduce | flops 2048 | bytes 16384 | tf_op jit(solution)/shard_map/psum | solution.py:103
  259.2 0.6 dynamic_slice.3
  (29 shorter events, 0.4 us)
Async XLA Ops:
  7.2 28.1 %copy-start = (bf16[32,1536]{1,0:T(8,128)(2,1)S(1)}, bf16[32,1536]{1,0:T(8,128)(2,1)}, u32[]{:S(2)}) copy-start(bf16[32,1536]{1,0:T(8,128)(2,1)} %param.11) | copy-start | bytes 294916
  34.9 17.4 %copy-start.2 = (bf16[32,6144]{1,0:T(8,128)(2,1)S(1)}, bf16[32,6144]{1,0:T(8,128)(2,1)}, u32[]{:S(2)}) copy-start(bf16[32,6144]{1,0:T(8,128)(2,1)} %param.16) | copy-start | bytes 1179652
  35.2 17.3 %copy-start.3 = (bf16[32,6144]{1,0:T(8,128)(2,1)S(1)}, bf16[32,6144]{1,0:T(8,128)(2,1)}, u32[]{:S(2)}) copy-start(bf16[32,6144]{1,0:T(8,128)(2,1)} %param.15) | copy-start | bytes 1179652
  35.3 17.3 %copy-start.4 = (bf16[32,6144]{1,0:T(8,128)(2,1)S(1)}, bf16[32,6144]{1,0:T(8,128)(2,1)}, u32[]{:S(2)}) copy-start(bf16[32,6144]{1,0:T(8,128)(2,1)} %param.17) | copy-start | bytes 1179652
  47.4 10.9 %all-to-all-start = ((bf16[4,8,1536]{2,1,0:T(8,128)(2,1)}), bf16[4,8,1536]{2,1,0:T(8,128)(2,1)S(1)}, u32[]{:S(2)}, u32[]{:S(2)}) async-start(bf16[4,8,1536]{2,1,0:T(8,128)(2,1)} %convert_element_type.30), calls=%async_computation | async-start | bytes 196608 | tf_op jit(solution)/shard_map/all_to_all | solution.py:87
  52.3 104.9 %all-gather.2.cloned.1.call-start = ((), (), s32[]{:S(2)}) async-start(), calls=%async_computation.1 | async-start | bytes 12976128 | tf_op jit(solution)/shard_map/all_gather | solution.py:92
  60.2 1.4 copy-start.1
  60.2 1.7 copy-start.5
  61.5 1.5 copy-start.6
Sparse Core Ops, SparseCore 0:
  63.1 94.0 all-gather.1
where the time goes:
time: 267 us
  blocking collectives  114 us (43%)
  waiting for transfers between devices  98.9 us (37%)
  matrix products  22.3 us (8%)
  between operations  14.9 us (6%)
  other arithmetic  6.73 us (3%)
  starting transfers between devices  4.87 us (2%)
  local copies, waits for them, and re-layouts  4.72 us (2%)
    all_gather x1, waiting for transfers between devices, local(): piece = lax.all_gather(hidden, ('ctx', 'vocab'), axis=0, tiled=True)  93.5 us
    psum x1, blocking collectives, local(): lax.psum((stats[1] * jnp.exp(stats[0] - peaks), stats[2]), ('ctx', 'vocab'))  40.7 us
    pmax x1, blocking collectives, local(): peaks = lax.pmax(stats[0], ('ctx', 'vocab'))  38.6 us
    dot_general x1, matrix products, local(): logits = jnp.dot(piece, head_weight, preferred_element_type=jnp.float32)  19.4 us
    unnamed x1, blocking collectives  15.1 us
    all_gather x1, blocking collectives, local(): values = lax.all_gather(block_value, 'ctx', axis=0, tiled=True)  10.1 us
    all_gather x1, blocking collectives, local(): keys = lax.all_gather(block_key, 'ctx', axis=0, tiled=True)  9.77 us
    all_to_all x1, waiting for transfers between devices, local(): lax.all_to_all(block_context, 'vocab', split_axis=0, concat_axis=1, tiled...  5.35 us
  transfers between devices with their start and end apart: 2, of which 2 were waited for; matrix products, arithmetic and copies ran while one was open for 0% of the time, Pallas kernels for 0%

commit v1 on v0

--- a/solution.py
+++ b/solution.py
@@ -1,13 +1,16 @@
+import functools
 import math
 
 import jax
 import jax.numpy as jnp
 from jax import lax
+from jax.experimental import pallas as pl
+from jax.experimental.pallas import tpu as pltpu
 from jax.sharding import PartitionSpec as P
 
 HEAD_DIM = 128
 BLOCK_LEN = 4
-
+MESH = pl.DeviceIdType.MESH
 
 big_negative = -1e30
 
@@ -42,7 +45,270 @@
     return (summed * lax.rsqrt(power + 1e-05) * norm_gain).astype(jnp.bfloat16)
 
 
+class Place:
+    def __init__(self, ctx_size, vocab_size):
+        self.nv = vocab_size
+        self.chips = ctx_size // 2
+        self.bits = [1 << i for i in range(self.chips.bit_length() - 1)]
+        assert ctx_size == 2 << len(self.bits) and vocab_size % 2 == 0
+        self.ctx = lax.axis_index("ctx")
+        self.z = lax.axis_index("vocab")
+
+    def flip(self, mask):
+        ctx, out, bit = self.ctx, self.ctx, 1
+        while bit <= mask:
+            if mask & bit:
+                has = lax.rem(lax.div(ctx, bit), 2)
+                out = out + bit - 2 * bit * has
+            bit *= 2
+        return out
+
+    def device(self, r, s, c):
+        return (self.flip(2 * r + c), lax.rem(self.z + (self.nv - s) % self.nv, self.nv))
+
+    def slot(self, r, s, c):
+        return (r * self.nv + s) * 2 + c
+
+    def onward(self, r, half):
+        if r == 0:
+            return list(self.bits)
+        if half == 0:
+            return [b for b in self.bits if b > r]
+        return [b for b in self.bits if b < (r & -r)]
+
+
+def entry_barrier(place):
+    barrier = pltpu.get_barrier_semaphore()
+    count = 0
+    for r in range(place.chips):
+        for s in range(place.nv):
+            for c in range(2):
+                if r or s or c:
+                    pl.semaphore_signal(
+                        barrier, inc=1, device_id=place.device(r, s, c), device_id_type=MESH
+                    )
+                    count += 1
+    pl.semaphore_wait(barrier, count)
+
+
+def head_kernel(
+    sizes, h_ref, w_hbm, t_ref, o_ref, rows, w_ref, logits, t_col, s_out, s_in,
+    w_sem, send, recv, s_send, s_recv,
+):
+    place = Place(*sizes)
+    nv, chips = place.nv, place.chips
+    tok, width = h_ref.shape
+    cols = w_ref.shape[1]
+    half_width = width // 2
+    per_group = nv * 2
+    group = per_group * tok
+    load_w = pltpu.make_async_copy(w_hbm, w_ref, w_sem)
+    load_w.start()
+    rows[pl.ds(0, tok), :] = h_ref[...]
+    entry_barrier(place)
+
+    sent = []
+
+    def view(slot, half):
+        return rows.at[pl.ds(slot * tok, tok), pl.ds(half * half_width, half_width)]
+
+    def push(src, half, dst, device):
+        dst_slot = place.slot(*dst)
+        copy = pltpu.make_async_remote_copy(
+            src_ref=view(place.slot(*src), half),
+            dst_ref=view(dst_slot, half),
+            send_sem=send.at[len(sent)],
+            recv_sem=recv.at[2 * dst_slot + half],
+            device_id=device,
+            device_id_type=MESH,
+        )
+        copy.start()
+        sent.append(copy)
+
+    def arrived(r, s, c, half):
+        slot = place.slot(r, s, c)
+        pltpu.make_async_copy(view(slot, half), view(slot, half), recv.at[2 * slot + half]).wait()
+
+    def along_vocab(s, half):
+        mid = nv // 2
+        ahead = s < mid - 1 or (s == mid - 1 and half == 0)
+        back = s == 0 or s > mid + 1 or (s == mid + 1 and half == 1)
+        if s == 0:
+            ahead = mid > 1 or half == 0
+            back = mid > 1 or half == 1
+        if ahead:
+            push((0, s, 0), half, (0, s + 1, 0), place.device(0, nv - 1, 0))
+        if back:
+            push((0, s, 0), half, (0, (s - 1) % nv, 0), place.device(0, 1, 0))
+
+    def pass_on(r, s, half):
+        if r == 0:
+            along_vocab(s, half)
+        for bit in place.onward(r, half):
+            push((r, s, 0), half, (r ^ bit, s, 0), place.device(bit, 0, 0))
+        push((r, s, 0), half, (r, s, 1), place.device(0, 0, 1))
+
+    order = [0]
+    for d in range(1, nv // 2):
+        order += [d, nv - d]
+    order.append(nv // 2)
+
+    def take(r, s):
+        for half in range(2):
+            if r or s:
+                arrived(r, s, 0, half)
+            pass_on(r, s, half)
+
+    for half in range(2):
+        along_vocab(0, half)
+    for half in range(2):
+        for bit in place.bits:
+            push((0, 0, 0), half, (bit, 0, 0), place.device(bit, 0, 0))
+    for half in range(2):
+        push((0, 0, 0), half, (0, 0, 1), place.device(0, 0, 1))
+
+    first = place.ctx * nv + place.z
+
+    def place_targets(r):
+        for s in range(nv):
+            for c in range(2):
+                ctx, z = place.device(r, s, c)
+                start = pl.multiple_of((ctx * nv + z) * tok, tok)
+                t_col[pl.ds(place.slot(r, s, c) * tok, tok), :] = t_ref[pl.ds(start, tok), :]
+
+    for r in range(chips):
+        place_targets(r)
+
+    s_sent = []
+    lane = lax.broadcasted_iota(jnp.int32, (tok, 128), 1)
+    column = lax.broadcasted_iota(jnp.int32, (tok, cols), 1) + first * cols
+    tile = min(256, cols)
+
+    def compute(r):
+        for s in range(nv):
+            for half in range(2):
+                arrived(r, s, 1, half)
+        base = r * group
+
+        @pl.loop(0, cols // tile)
+        def _(n):
+            at = pl.ds(pl.multiple_of(n * tile, tile), tile)
+            logits[:, at] = jnp.dot(
+                rows[pl.ds(base, group), :], w_ref[:, at], preferred_element_type=jnp.float32
+            )
+
+        @pl.loop(0, per_group)
+        def _(i):
+            at = pl.multiple_of(i * tok, tok)
+            block = logits[pl.ds(at, tok), :]
+            top = jnp.max(block, axis=1, keepdims=True)
+            mass = jnp.sum(jnp.exp(block - top), axis=1, keepdims=True)
+            wanted = t_col[pl.ds(pl.multiple_of(base + at, tok), tok), :]
+            pick = jnp.sum(jnp.where(column == wanted, block, 0.0), axis=1, keepdims=True)
+            packed = jnp.where(lane == 0, top, jnp.where(lane == 1, mass, pick))
+            if tok < 128:
+                packed = jnp.concatenate(
+                    [packed, jnp.zeros((128 - tok, 128), jnp.float32)], axis=0
+                )
+            s_out[r * per_group + i] = jnp.transpose(packed)[0:8, :]
+
+        for s in range(nv):
+            for c in range(2):
+                slot, there = place.slot(r, s, c), place.slot(r, (nv - s) % nv, c)
+                if r or s or c:
+                    copy = pltpu.make_async_remote_copy(
+                        src_ref=s_out.at[slot],
+                        dst_ref=s_in.at[there],
+                        send_sem=s_send.at[slot],
+                        recv_sem=s_recv.at[there],
+                        device_id=place.device(r, s, c),
+                        device_id_type=MESH,
+                    )
+                    copy.start()
+                    s_sent.append(copy)
+                else:
+                    s_in[0] = s_out[0]
+
+    outer = list(range(1, chips))
+    outer.sort(key=lambda r: (bin(r).count("1"), r))
+    near = [r for r in outer if r in place.bits]
+    far = [r for r in outer if r not in place.bits]
+    for r in near:
+        take(r, 0)
+    for s in order[1:]:
+        take(0, s)
+    for r in far:
+        take(r, 0)
+    for r in near:
+        for s in order[1:-1]:
+            take(r, s)
+    load_w.wait()
+    compute(0)
+    for r in near:
+        take(r, order[-1])
+    for r in far:
+        for s in order[1:-1]:
+            take(r, s)
+    for r in near:
+        compute(r)
+    for r in far:
+        take(r, order[-1])
+    for r in far:
+        compute(r)
+
+    for copy in s_sent:
+        copy.wait_recv()
+    stats = s_in[...]
+    tops = stats[:, 0:1, :]
+    top = jnp.max(tops, axis=0)
+    mass = jnp.sum(stats[:, 1:2, :] * jnp.exp(tops - top[None]), axis=0)
+    pick = jnp.sum(stats[:, 2:3, :], axis=0)
+    prior = pick - (top + jnp.log(mass))
+    o_ref[...] = prior
+    for copy in s_sent:
+        copy.wait_send()
+    for copy in sent:
+        copy.wait_send()
+
+
+def head_priors(sizes, hidden, head_weight, targets):
+    ctx_size, nv = sizes
+    tok, width = hidden.shape
+    cols = head_weight.shape[1]
+    devices = ctx_size * nv
+    tokens = devices * tok
+    out = pl.pallas_call(
+        functools.partial(head_kernel, sizes),
+        out_shape=jax.ShapeDtypeStruct((1, 128), jnp.float32),
+        in_specs=[
+            pl.BlockSpec(memory_space=pltpu.VMEM),
+            pl.BlockSpec(memory_space=pl.ANY),
+            pl.BlockSpec(memory_space=pltpu.VMEM),
+        ],
+        out_specs=pl.BlockSpec(memory_space=pltpu.VMEM),
+        scratch_shapes=[
+            pltpu.VMEM((tokens, width), jnp.bfloat16),
+            pltpu.VMEM((width, cols), jnp.bfloat16),
+            pltpu.VMEM((nv * 2 * tok, cols), jnp.float32),
+            pltpu.VMEM((tokens, 1), jnp.int32),
+            pltpu.VMEM((devices, 8, 128), jnp.float32),
+            pltpu.VMEM((devices, 8, 128), jnp.float32),
+            pltpu.SemaphoreType.DMA,
+            pltpu.SemaphoreType.DMA((2 * devices,)),
+            pltpu.SemaphoreType.DMA((2 * devices,)),
+            pltpu.SemaphoreType.DMA((devices,)),
+            pltpu.SemaphoreType.DMA((devices,)),
+        ],
+        compiler_params=pltpu.CompilerParams(
+            collective_id=0, has_side_effects=True, vmem_limit_bytes=58 * 1024 * 1024
+        ),
+        name="head_priors",
+    )(hidden, head_weight, targets.reshape(tokens, 1))
+    return out[0, :tok]
+
+
 def local(
+    sizes,
     block_query,
     block_key,
     block_value,
@@ -62,7 +328,6 @@
     queries = block_query.reshape(local_rows, head_count, HEAD_DIM)
     own_doc = block_doc.astype(jnp.bfloat16)
     query_places = first_row + jnp.arange(local_rows, dtype=jnp.int32)
-    highest = jnp.full((local_rows, head_count), big_negative, jnp.float32)
     keys = lax.all_gather(block_key, "ctx", axis=0, tiled=True)
     values = lax.all_gather(block_value, "ctx", axis=0, tiled=True)
     docs = lax.all_gather(own_doc, "ctx", axis=0, tiled=True)
@@ -73,40 +338,18 @@
     key_places = jnp.arange(count, dtype=jnp.int32)
     allowed = (query_places[:, None] >= key_places[None, :]) & (own_doc[:, None] == docs[None, :])
     allowed = allowed[:, None, :]
-    newest = jnp.maximum(highest, jnp.max(jnp.where(allowed, scores, big_negative), axis=-1))
+    newest = jnp.max(jnp.where(allowed, scores, big_negative), axis=-1)
     weights = jnp.where(allowed, jnp.exp(scores - newest[..., None]), 0.0)
     totals = jnp.sum(weights, axis=-1)
-    update = jnp.einsum(
+    mixed = jnp.einsum(
         "qhk,khd->qhd", weights.astype(jnp.bfloat16), values, preferred_element_type=jnp.float32
     )
-    mixed = update
-    highest, totals, mixed = (newest, totals, mixed)
     block_context = (
         (mixed / totals[..., None]).reshape(local_rows, head_count * HEAD_DIM).astype(jnp.bfloat16)
     )
     grouped = lax.all_to_all(block_context, "vocab", split_axis=0, concat_axis=1, tiled=True)
     hidden = local_decoder(grouped, token_query, token_key, token_value, token_state, norm_gain)
-    vocab_cols = head_weight.shape[1]
-    col_start = lax.axis_index(("ctx", "vocab")) * vocab_cols
-    columns = jnp.arange(vocab_cols, dtype=jnp.int32)
-    piece = lax.all_gather(hidden, ("ctx", "vocab"), axis=0, tiled=True)
-    logits = jnp.dot(piece, head_weight, preferred_element_type=jnp.float32)
-    top = jnp.max(logits, axis=-1)
-    mass = jnp.sum(jnp.exp(logits - top[:, None]), axis=-1)
-    wanted = targets - col_start
-    picked = jnp.sum(jnp.where(columns[None, :] == wanted[:, None], logits, 0.0), axis=1)
-    peaks = top
-    masses = mass
-    picks = picked
-    stats = (peaks, masses, picks)
-    peaks = lax.pmax(stats[0], ("ctx", "vocab"))
-    masses, picks = lax.psum((stats[1] * jnp.exp(stats[0] - peaks), stats[2]), ("ctx", "vocab"))
-    priors = picks - (peaks + jnp.log(masses))
-    own_count = hidden.shape[0]
-    token_prior = lax.dynamic_slice_in_dim(
-        priors, lax.axis_index(("ctx", "vocab")) * own_count, own_count
-    )
-    return (block_context, token_prior)
+    return (block_context, head_priors(sizes, hidden, head_weight, targets))
 
 
 def solution(mesh):
@@ -124,7 +367,7 @@
         P(),
     )
     return jax.shard_map(
-        local,
+        functools.partial(local, (mesh.shape["ctx"], mesh.shape["vocab"])),
         mesh=mesh,
         in_specs=placed,
         out_specs=(P("ctx", "vocab"), P(("ctx", "vocab"))),

time: 267 us -> 141 us (0.53)
  waiting for transfers between devices: 98.9 us -> 3.48 us
  Pallas kernels: 0 us -> 82.6 us
  blocking collectives: 114 us -> 34.9 us
  matrix products: 22.3 us -> 2.79 us
  between operations: 14.9 us -> 1.52 us
  other arithmetic: 6.73 us -> 3.4 us
  local copies, waits for them, and re-layouts: 4.72 us -> 7.39 us
    all_gather x1 -> x0, waiting for transfers between devices: 93.5 us -> none  [local(): piece = lax.all_gather(hidden, ('ctx', 'vocab'), axis=0, tiled=True)]
    pallas_call x0 -> x1, Pallas kernels: none -> 82.6 us  [head_priors(): pl.pallas_call(functools.partial(head_kernel, sizes), out_shape=jax.Shape...]
    psum x1 -> x0, blocking collectives: 40.7 us -> none  [local(): lax.psum((stats[1] * jnp.exp(stats[0] - peaks), stats[2]), ('ctx', 'vocab'))]
    pmax x1 -> x0, blocking collectives: 38.6 us -> none  [local(): peaks = lax.pmax(stats[0], ('ctx', 'vocab'))]
    dot_general x1 -> x0, matrix products: 19.4 us -> none  [local(): logits = jnp.dot(piece, head_weight, preferred_element_type=jnp.float32)]
    reduce_sum x2 -> x0, other arithmetic: 3.53 us -> none  [the longest x1 3.3 us: local(): mass = jnp.sum(jnp.exp(logits - top[:, None]), axis=-1)]
  transfers between devices with their start and end apart: 2 -> 1, of which waited for: 2 -> 1; matrix products, arithmetic and copies ran while one was open for 0% -> 2% of each run, Pallas kernels for 0% -> 0%
where the time goes in v1:
time: 141 us
  Pallas kernels  82.6 us (59%)
  blocking collectives  34.9 us (25%)
  local copies, waits for them, and re-layouts  7.39 us (5%)
  starting transfers between devices  4.88 us (3%)
  waiting for transfers between devices  3.48 us (2%)
  other arithmetic  3.4 us (2%)
  matrix products  2.79 us (2%)
  between operations  1.52 us (1%)
    pallas_call x1, Pallas kernels, head_priors(): pl.pallas_call(functools.partial(head_kernel, sizes), out_shape=jax.Shape...  82.6 us
    unnamed x1, blocking collectives  15.1 us
    all_gather x1, blocking collectives, local(): values = lax.all_gather(block_value, 'ctx', axis=0, tiled=True)  10 us
    all_gather x1, blocking collectives, local(): keys = lax.all_gather(block_key, 'ctx', axis=0, tiled=True)  9.77 us
    all_to_all x1, starting transfers between devices, local(): lax.all_to_all(block_context, 'vocab', split_axis=0, concat_axis=1, tiled...  4.88 us
    all_to_all x1, waiting for transfers between devices, local(): lax.all_to_all(block_context, 'vocab', split_axis=0, concat_axis=1, tiled...  3.48 us
  transfers between devices with their start and end apart: 1, of which 1 were waited for; matrix products, arithmetic and copies ran while one was open for 2% of the time, Pallas kernels for 0%

profile of v1, /device:TPU:0, one launch (start us, length us, event | category | flops | bytes accessed | tf_op | source)
XLA Modules:
  0.0 141.0 jit_solution(11604033339043151088)
XLA Ops:
  0.7 0.7 convert_element_type.25
  1.4 1.2 dynamic-slice
  3.3 0.2 dynamic-update-slice
  3.5 15.1 %all-reduce = bf16[256]{0:T(256)(128)(2,1)S(1)} all-reduce(bf16[256]{0:T(256)(128)(2,1)S(1)} %dynamic-update-slice), channel_id=1, replica_groups=mesh['ctx'=8,'vocab'=4] {'ctx'}, use_global_device_ids=true, to_apply=%add | all-reduce | flops 256 | bytes 1024
  18.6 9.8 %all_gather.10 = bf16[256,1536]{1,0:T(8,128)(2,1)S(1)} all-gather(bf16[32,1536]{1,0:T(8,128)(2,1)} %param.12), channel_id=1, replica_groups=mesh['ctx'=8,'vocab'=4] {'ctx'}, dimensions={0}, use_global_device_ids=true | all-gather | bytes 884736 | tf_op jit(solution)/shard_map/all_gather | solution.py:331
  28.4 0.3 copy.31
  28.7 10.0 %all_gather.11 = bf16[256,1536]{1,0:T(8,128)(2,1)S(1)} all-gather(bf16[32,1536]{1,0:T(8,128)(2,1)S(1)} %copy-done.5), channel_id=1, replica_groups=mesh['ctx'=8,'vocab'=4] {'ctx'}, dimensions={0}, use_global_device_ids=true | all-gather | bytes 884736 | tf_op jit(solution)/shard_map/all_gather | solution.py:332
  38.8 0.3 copy.34
  39.0 0.1 fusion.27
  39.1 0.2 fusion.7
  39.4 0.2 fusion.35
  39.6 0.4 fusion.9
  40.1 0.7 convert_element_type.30
  40.8 4.9 %all-to-all-start = ((bf16[4,8,1536]{2,1,0:T(8,128)(2,1)}), bf16[4,8,1536]{2,1,0:T(8,128)(2,1)S(1)}, u32[]{:S(2)}, u32[]{:S(2)}) async-start(bf16[4,8,1536]{2,1,0:T(8,128)(2,1)} %convert_element_type.30), calls=%async_computation | async-start | bytes 196608 | tf_op jit(solution)/shard_map/all_to_all | solution.py:350
  45.7 0.6 copy_bitcast_fusion
  46.4 0.2 copy.42
  46.6 0.1 copy.52
  46.7 0.1 copy.50
  46.7 0.2 copy.40
  46.9 0.2 copy-done.7
  47.1 1.0 copy.45.t_ref
  48.1 0.1 iota_compare_fusion.1
  48.2 3.5 %all-to-all-done = bf16[4,8,1536]{2,1,0:T(8,128)(2,1)S(1)} async-done(((bf16[4,8,1536]{2,1,0:T(8,128)(2,1)}), bf16[4,8,1536]{2,1,0:T(8,128)(2,1)S(1)}, u32[]{:S(2)}, u32[]{:S(2)}) %all-to-all-start) | async-done | bytes 98336 | tf_op jit(solution)/shard_map/all_to_all | solution.py:350
  51.8 0.9 fusion.36
  52.7 0.9 fusion.12
  53.6 1.2 fusion.3
  54.9 0.1 copy.44
  55.0 0.9 copy-done.1
  55.9 0.4 multiply_reduce_fusion
  56.2 1.0 multiply_convert_fusion.h_ref
  57.3 82.6 %head_priors.1 = f32[1,128]{1,0:T(1,128)} custom-call(bf16[32,6144]{1,0:T(8,128)(2,1)} %multiply_convert_fusion.h_ref, bf16[6144,1024]{1,0:T(8,128)(2,1)} %w_hbm.1, s32[1024,1]{1,0:T(8,128)} %copy.45.t_ref), custom_call_target="tpu_custom_call" | custom-call | tf_op jit(solution)/shard_map/head_priors/pallas_call | solution.py:280
  139.9 1.1 slice_bitcast_fusion
  (22 shorter events, 0.3 us)
Async XLA Ops:
  0.6 38.5 %copy-start = (bf16[32,1536]{1,0:T(8,128)(2,1)S(1)}, bf16[32,1536]{1,0:T(8,128)(2,1)}, u32[]{:S(2)}) copy-start(bf16[32,1536]{1,0:T(8,128)(2,1)} %param.11) | copy-start | bytes 294916
  0.6 28.1 %copy-start.5 = (bf16[32,1536]{1,0:T(8,128)(2,1)S(1)}, bf16[32,1536]{1,0:T(8,128)(2,1)}, u32[]{:S(2)}) copy-start(bf16[32,1536]{1,0:T(8,128)(2,1)} %param.13) | copy-start | bytes 294916
  39.4 7.0 %copy-start.2 = (bf16[32,6144]{1,0:T(8,128)(2,1)S(1)}, bf16[32,6144]{1,0:T(8,128)(2,1)}, u32[]{:S(2)}) copy-start(bf16[32,6144]{1,0:T(8,128)(2,1)} %param.16) | copy-start | bytes 1179652
  40.0 6.6 %copy-start.3 = (bf16[32,6144]{1,0:T(8,128)(2,1)S(1)}, bf16[32,6144]{1,0:T(8,128)(2,1)}, u32[]{:S(2)}) copy-start(bf16[32,6144]{1,0:T(8,128)(2,1)} %param.15) | copy-start | bytes 1179652
  40.0 6.6 %copy-start.4 = (bf16[32,6144]{1,0:T(8,128)(2,1)S(1)}, bf16[32,6144]{1,0:T(8,128)(2,1)}, u32[]{:S(2)}) copy-start(bf16[32,6144]{1,0:T(8,128)(2,1)} %param.17) | copy-start | bytes 1179652
  40.8 10.9 %all-to-all-start = ((bf16[4,8,1536]{2,1,0:T(8,128)(2,1)}), bf16[4,8,1536]{2,1,0:T(8,128)(2,1)S(1)}, u32[]{:S(2)}, u32[]{:S(2)}) async-start(bf16[4,8,1536]{2,1,0:T(8,128)(2,1)} %convert_element_type.30), calls=%async_computation | async-start | bytes 196608 | tf_op jit(solution)/shard_map/all_to_all | solution.py:350
  46.4 0.7 copy-start.7
  54.9 1.0 copy-start.1
  54.9 1.3 copy-start.6

commit v2 on v1

--- a/solution.py
+++ b/solution.py
@@ -13,36 +13,6 @@
 MESH = pl.DeviceIdType.MESH
 
 big_negative = -1e30
-
-
-def local_decoder(context, token_query, token_key, token_value, token_state, norm_gain):
-    scale = 1.0 / math.sqrt(HEAD_DIM)
-    groups = context.shape[0]
-    width = context.shape[1]
-    head_total = width // HEAD_DIM
-    shape = (groups, BLOCK_LEN, head_total, HEAD_DIM)
-    prefix = context.reshape(groups, 1, head_total, HEAD_DIM)
-    queries = token_query.reshape(shape)
-    keys = jnp.concatenate([prefix, token_key.reshape(shape)], axis=1)
-    values = jnp.concatenate([prefix, token_value.reshape(shape)], axis=1)
-    scores = (
-        jnp.einsum("bihd,bjhd->bhij", queries, keys, preferred_element_type=jnp.float32) * scale
-    )
-    allowed = (
-        jnp.arange(BLOCK_LEN + 1, dtype=jnp.int32)[None, :]
-        <= jnp.arange(BLOCK_LEN, dtype=jnp.int32)[:, None] + 1
-    )
-    scores = jnp.where(allowed, scores, -jnp.inf)
-    highest = jnp.max(scores, axis=-1, keepdims=True)
-    weights = jnp.exp(scores - highest)
-    totals = jnp.sum(weights, axis=-1)
-    mixed = jnp.einsum(
-        "bhij,bjhd->bihd", weights.astype(jnp.bfloat16), values, preferred_element_type=jnp.float32
-    )
-    mixed = mixed / jnp.transpose(totals, (0, 2, 1))[..., None]
-    summed = token_state.astype(jnp.float32) + mixed.reshape(groups * BLOCK_LEN, width)
-    power = jnp.mean(summed * summed, axis=-1, keepdims=True)
-    return (summed * lax.rsqrt(power + 1e-05) * norm_gain).astype(jnp.bfloat16)
 
 
 class Place:
@@ -91,21 +61,217 @@
     pl.semaphore_wait(barrier, count)
 
 
-def head_kernel(
-    sizes, h_ref, w_hbm, t_ref, o_ref, rows, w_ref, logits, t_col, s_out, s_in,
+def up_to(value, unit):
+    return (value + unit - 1) // unit * unit
+
+
+def kernel(
+    sizes, bq_hbm, bk_hbm, bv_hbm, doc_ref, tq_hbm, tk_hbm, tv_hbm, ts_hbm, g_ref, w_hbm, t_ref,
+    bc_ref, o_ref,
+    bq, kv, doc_in, c_all, c_out, c_in, tq, kcat, vcat, ts, summed,
+    rows, w_ref, logits, t_col, s_out, s_in,
+    in_sems, kv_send, kv_recv, d_send, d_recv, c_send, c_recv,
     w_sem, send, recv, s_send, s_recv,
 ):
     place = Place(*sizes)
     nv, chips = place.nv, place.chips
-    tok, width = h_ref.shape
+    tok, width = ts.shape
     cols = w_ref.shape[1]
     half_width = width // 2
     per_group = nv * 2
     group = per_group * tok
+    blk, part = bq.shape
+    scale = 1.0 / math.sqrt(HEAD_DIM)
+    heads = part // HEAD_DIM
+    share = blk // nv
+    pad8, pad16 = up_to(share, 8), up_to(share, 16)
+
+    loads = [
+        pltpu.make_async_copy(bk_hbm, kv.at[0, pl.ds(0, blk)], in_sems.at[0]),
+        pltpu.make_async_copy(bv_hbm, kv.at[1, pl.ds(0, blk)], in_sems.at[1]),
+        pltpu.make_async_copy(bq_hbm, bq, in_sems.at[2]),
+        pltpu.make_async_copy(tq_hbm, tq, in_sems.at[3]),
+        pltpu.make_async_copy(tk_hbm, kcat.at[pl.ds(0, tok)], in_sems.at[4]),
+        pltpu.make_async_copy(tv_hbm, vcat.at[pl.ds(0, tok)], in_sems.at[5]),
+        pltpu.make_async_copy(ts_hbm, ts, in_sems.at[6]),
+    ]
+    for load in loads:
+        load.start()
     load_w = pltpu.make_async_copy(w_hbm, w_ref, w_sem)
     load_w.start()
-    rows[pl.ds(0, tok), :] = h_ref[...]
+
+    lane8 = lax.broadcasted_iota(jnp.int32, (8, 128), 1)
+    doc_in[0] = jnp.zeros((8, 128), jnp.float32)
+    doc_in[0, 0:1, 0:blk] = doc_ref[...].astype(jnp.float32)
+    tiled = doc_in[0]
+    span = blk
+    while span < 128:
+        tiled = tiled + pltpu.roll(tiled, span, 1)
+        span *= 2
+    doc_in[0] = tiled
     entry_barrier(place)
+
+    kv_sent = []
+
+    def kv_view(r, c, half):
+        return kv.at[half, pl.ds((2 * r + c) * blk, blk)]
+
+    def kv_push(src, half, dst, device):
+        copy = pltpu.make_async_remote_copy(
+            src_ref=kv_view(*src, half),
+            dst_ref=kv_view(*dst, half),
+            send_sem=kv_send.at[len(kv_sent)],
+            recv_sem=kv_recv.at[2 * (2 * dst[0] + dst[1]) + half],
+            device_id=device,
+            device_id_type=MESH,
+        )
+        copy.start()
+        kv_sent.append(copy)
+
+    def kv_arrived(r, c, half):
+        ref = kv_view(r, c, half)
+        pltpu.make_async_copy(ref, ref, kv_recv.at[2 * (2 * r + c) + half]).wait()
+
+    def kv_pass(r, half):
+        for bit in place.onward(r, half):
+            kv_push((r, 0), half, (r ^ bit, 0), place.device(bit, 0, 0))
+        kv_push((r, 0), half, (r, 1), place.device(0, 0, 1))
+
+    nearest = sorted(range(1, chips), key=lambda r: (bin(r).count("1"), r))
+    for half in range(2):
+        loads[half].wait()
+        kv_pass(0, half)
+    d_sent = []
+    for r in range(chips):
+        for c in range(2):
+            slot = 2 * r + c
+            if slot:
+                copy = pltpu.make_async_remote_copy(
+                    src_ref=doc_in.at[0],
+                    dst_ref=doc_in.at[slot],
+                    send_sem=d_send.at[slot],
+                    recv_sem=d_recv.at[slot],
+                    device_id=place.device(r, 0, c),
+                    device_id_type=MESH,
+                )
+                copy.start()
+                d_sent.append(copy)
+
+    t_lane = lax.broadcasted_iota(jnp.int32, (tok, 128), 1)
+    t_row = lax.broadcasted_iota(jnp.int32, (tok, 128), 0)
+    in_row = 128 // tok
+    for r in range(chips):
+        for s in range(nv):
+            for c in range(2):
+                ctx, z = place.device(r, s, c)
+                flat = ctx * nv + z
+                line = t_ref[pl.ds(lax.div(flat, in_row), 1), :].astype(jnp.float32)
+                here = t_lane == t_row + lax.rem(flat, in_row) * tok
+                t_col[pl.ds(place.slot(r, s, c) * tok, tok), :] = jnp.sum(
+                    jnp.where(here, line, 0.0), axis=1, keepdims=True
+                )
+
+    for r in nearest:
+        for half in range(2):
+            kv_arrived(r, 0, half)
+            kv_pass(r, half)
+
+    q_lane = lax.broadcasted_iota(jnp.int32, (blk, 128), 1)
+    q_row = lax.broadcasted_iota(jnp.int32, (blk, 128), 0)
+    own_doc = jnp.sum(jnp.where(q_lane == q_row, tiled[0:1, :], 0.0), axis=1, keepdims=True)
+    own_place = q_row + place.ctx * blk
+    for copy in d_sent:
+        copy.wait_recv()
+    masks = []
+    fit = 128 // blk
+    for first in range(0, 2 * chips, fit):
+        docs = jnp.zeros((1, 128), jnp.float32)
+        places = jnp.zeros((blk, 128), jnp.int32)
+        for k in range(fit):
+            slot = first + k
+            mine = (q_lane >= k * blk) & (q_lane < (k + 1) * blk)
+            docs = jnp.where(mine[0:1, :], doc_in[slot, 0:1, :], docs)
+            places = jnp.where(mine, place.flip(slot) * blk - k * blk + q_lane, places)
+        masks.append(((own_doc == docs) & (own_place >= places)).astype(jnp.float32))
+    allowed = (jnp.concatenate(masks, axis=1) > 0.5)[None]
+    loads[2].wait()
+    for r in range(chips):
+        for half in range(2):
+            kv_arrived(r, 1, half)
+
+    def softmax(scores, allowed):
+        scores = jnp.where(allowed, scores * scale, big_negative)
+        top = jnp.max(scores, axis=-1, keepdims=True)
+        weights = jnp.where(allowed, jnp.exp(scores - top), 0.0)
+        return weights.astype(jnp.bfloat16), jnp.sum(weights, axis=-1, keepdims=True)
+
+    def dot_t(a, b):
+        return lax.dot_general(a, b, (((1,), (1,)), ((), ())), preferred_element_type=jnp.float32)
+
+    ats = [pl.ds(h * HEAD_DIM, HEAD_DIM) for h in range(heads)]
+    scores = jnp.stack([dot_t(bq[:, at], kv[0, :, at]) for at in ats])
+    weights, totals = softmax(scores, allowed)
+    if pad8 > share:
+        c_out[...] = jnp.zeros_like(c_out)
+    for h, at in enumerate(ats):
+        mixed = jnp.dot(weights[h], kv[1, :, at], preferred_element_type=jnp.float32) / totals[h]
+        rounded = mixed.astype(jnp.bfloat16)
+        bc_ref[:, at] = rounded
+        c_all[:, at] = rounded.astype(jnp.float32)
+    for v in range(nv):
+        c_out[v, 0:share, :] = c_all[v * share:(v + 1) * share, :]
+
+    c_sent = []
+    for s in sorted(range(1, nv), key=lambda s: -min(s, nv - s)):
+        device = place.device(0, s, 0)
+        copy = pltpu.make_async_remote_copy(
+            src_ref=c_out.at[device[1]],
+            dst_ref=c_in.at[place.z],
+            send_sem=c_send.at[s],
+            recv_sem=c_recv.at[s],
+            device_id=device,
+            device_id_type=MESH,
+        )
+        copy.start()
+        c_sent.append(copy)
+    c_in[place.z] = c_out[place.z]
+
+    deep = tok + pad16
+    l_row = lax.broadcasted_iota(jnp.int32, (tok, deep), 0)
+    l_col = lax.broadcasted_iota(jnp.int32, (tok, deep), 1)
+    l_block = lax.div(l_row, BLOCK_LEN)
+    usable = (l_col < tok) & (l_col <= l_row) & (lax.div(l_col, BLOCK_LEN) == l_block)
+    usable = (usable | (l_col == tok + l_block))[None]
+    for load in loads[3:]:
+        load.wait()
+    for copy in c_sent:
+        copy.wait_recv()
+
+    def decode(v, power):
+        context = c_in[v]
+        if pad16 > pad8:
+            context = jnp.concatenate(
+                [context, jnp.zeros((pad16 - pad8, part), jnp.float32)], axis=0
+            )
+        context = context.astype(jnp.bfloat16)
+        start = pl.multiple_of(v * part, part)
+        kcat[pl.ds(tok, pad16), pl.ds(start, part)] = context
+        vcat[pl.ds(tok, pad16), pl.ds(start, part)] = context
+        spots = [pl.ds(pl.multiple_of(start + h * HEAD_DIM, HEAD_DIM), HEAD_DIM) for h in range(heads)]
+        scores = jnp.stack([dot_t(tq[:, at], kcat[:, at]) for at in spots])
+        weights, totals = softmax(scores, usable)
+        for h, at in enumerate(spots):
+            mixed = jnp.dot(weights[h], vcat[:, at], preferred_element_type=jnp.float32)
+            total = ts[:, at].astype(jnp.float32) + mixed / totals[h]
+            summed[:, at] = total
+            power = power + total * total
+        return power
+
+    power = lax.fori_loop(0, nv, decode, jnp.zeros((tok, HEAD_DIM), jnp.float32))
+    power = jnp.sum(power, axis=1, keepdims=True) / width
+    rows[pl.ds(0, tok), :] = (
+        summed[...] * lax.rsqrt(power + 1e-05) * g_ref[...]
+    ).astype(jnp.bfloat16)
 
     sent = []
 
@@ -168,20 +334,10 @@
         push((0, 0, 0), half, (0, 0, 1), place.device(0, 0, 1))
 
     first = place.ctx * nv + place.z
-
-    def place_targets(r):
-        for s in range(nv):
-            for c in range(2):
-                ctx, z = place.device(r, s, c)
-                start = pl.multiple_of((ctx * nv + z) * tok, tok)
-                t_col[pl.ds(place.slot(r, s, c) * tok, tok), :] = t_ref[pl.ds(start, tok), :]
-
-    for r in range(chips):
-        place_targets(r)
-
     s_sent = []
     lane = lax.broadcasted_iota(jnp.int32, (tok, 128), 1)
     column = lax.broadcasted_iota(jnp.int32, (tok, cols), 1) + first * cols
+    column = column.astype(jnp.float32)
     tile = min(256, cols)
 
     def compute(r):
@@ -264,47 +420,11 @@
     mass = jnp.sum(stats[:, 1:2, :] * jnp.exp(tops - top[None]), axis=0)
     pick = jnp.sum(stats[:, 2:3, :], axis=0)
     prior = pick - (top + jnp.log(mass))
-    o_ref[...] = prior
+    o_ref[...] = prior[:, 0:tok]
     for copy in s_sent:
         copy.wait_send()
-    for copy in sent:
+    for copy in sent + kv_sent + d_sent + c_sent:
         copy.wait_send()
-
-
-def head_priors(sizes, hidden, head_weight, targets):
-    ctx_size, nv = sizes
-    tok, width = hidden.shape
-    cols = head_weight.shape[1]
-    devices = ctx_size * nv
-    tokens = devices * tok
-    out = pl.pallas_call(
-        functools.partial(head_kernel, sizes),
-        out_shape=jax.ShapeDtypeStruct((1, 128), jnp.float32),
-        in_specs=[
-            pl.BlockSpec(memory_space=pltpu.VMEM),
-            pl.BlockSpec(memory_space=pl.ANY),
-            pl.BlockSpec(memory_space=pltpu.VMEM),
-        ],
-        out_specs=pl.BlockSpec(memory_space=pltpu.VMEM),
-        scratch_shapes=[
-            pltpu.VMEM((tokens, width), jnp.bfloat16),
-            pltpu.VMEM((width, cols), jnp.bfloat16),
-            pltpu.VMEM((nv * 2 * tok, cols), jnp.float32),
-            pltpu.VMEM((tokens, 1), jnp.int32),
-            pltpu.VMEM((devices, 8, 128), jnp.float32),
-            pltpu.VMEM((devices, 8, 128), jnp.float32),
-            pltpu.SemaphoreType.DMA,
-            pltpu.SemaphoreType.DMA((2 * devices,)),
-            pltpu.SemaphoreType.DMA((2 * devices,)),
-            pltpu.SemaphoreType.DMA((devices,)),
-            pltpu.SemaphoreType.DMA((devices,)),
-        ],
-        compiler_params=pltpu.CompilerParams(
-            collective_id=0, has_side_effects=True, vmem_limit_bytes=58 * 1024 * 1024
-        ),
-        name="head_priors",
-    )(hidden, head_weight, targets.reshape(tokens, 1))
-    return out[0, :tok]
 
 
 def local(
@@ -321,35 +441,75 @@
     head_weight,
     targets,
 ):
-    local_rows = block_query.shape[0]
-    head_count = block_query.shape[1] // HEAD_DIM
-    scale = 1.0 / math.sqrt(HEAD_DIM)
-    first_row = lax.axis_index("ctx") * local_rows
-    queries = block_query.reshape(local_rows, head_count, HEAD_DIM)
-    own_doc = block_doc.astype(jnp.bfloat16)
-    query_places = first_row + jnp.arange(local_rows, dtype=jnp.int32)
-    keys = lax.all_gather(block_key, "ctx", axis=0, tiled=True)
-    values = lax.all_gather(block_value, "ctx", axis=0, tiled=True)
-    docs = lax.all_gather(own_doc, "ctx", axis=0, tiled=True)
-    count = keys.shape[0]
-    keys = keys.reshape(count, head_count, HEAD_DIM)
-    values = values.reshape(count, head_count, HEAD_DIM)
-    scores = jnp.einsum("qhd,khd->qhk", queries, keys, preferred_element_type=jnp.float32) * scale
-    key_places = jnp.arange(count, dtype=jnp.int32)
-    allowed = (query_places[:, None] >= key_places[None, :]) & (own_doc[:, None] == docs[None, :])
-    allowed = allowed[:, None, :]
-    newest = jnp.max(jnp.where(allowed, scores, big_negative), axis=-1)
-    weights = jnp.where(allowed, jnp.exp(scores - newest[..., None]), 0.0)
-    totals = jnp.sum(weights, axis=-1)
-    mixed = jnp.einsum(
-        "qhk,khd->qhd", weights.astype(jnp.bfloat16), values, preferred_element_type=jnp.float32
+    ctx_size, nv = sizes
+    blk, part = block_query.shape
+    tok, width = token_state.shape
+    cols = head_weight.shape[1]
+    devices = ctx_size * nv
+    tokens = devices * tok
+    share = blk // nv
+    pad8, pad16 = up_to(share, 8), up_to(share, 16)
+    vmem = pl.BlockSpec(memory_space=pltpu.VMEM)
+    hbm = pl.BlockSpec(memory_space=pl.ANY)
+    dma = pltpu.SemaphoreType.DMA
+    bf16, f32 = jnp.bfloat16, jnp.float32
+    context, prior = pl.pallas_call(
+        functools.partial(kernel, sizes),
+        out_shape=(
+            jax.ShapeDtypeStruct((blk, part), bf16),
+            jax.ShapeDtypeStruct((1, tok), f32),
+        ),
+        in_specs=[hbm, hbm, hbm, vmem, hbm, hbm, hbm, hbm, vmem, hbm, vmem],
+        out_specs=(vmem, vmem),
+        scratch_shapes=[
+            pltpu.VMEM((blk, part), bf16),
+            pltpu.VMEM((2, ctx_size * blk, part), bf16),
+            pltpu.VMEM((ctx_size, 8, 128), f32),
+            pltpu.VMEM((blk, part), f32),
+            pltpu.VMEM((nv, pad8, part), f32),
+            pltpu.VMEM((nv, pad8, part), f32),
+            pltpu.VMEM((tok, width), bf16),
+            pltpu.VMEM((tok + pad16, width), bf16),
+            pltpu.VMEM((tok + pad16, width), bf16),
+            pltpu.VMEM((tok, width), bf16),
+            pltpu.VMEM((tok, width), f32),
+            pltpu.VMEM((tokens, width), bf16),
+            pltpu.VMEM((width, cols), bf16),
+            pltpu.VMEM((nv * 2 * tok, cols), f32),
+            pltpu.VMEM((tokens, 1), f32),
+            pltpu.VMEM((devices, 8, 128), f32),
+            pltpu.VMEM((devices, 8, 128), f32),
+            dma((7,)),
+            dma((2 * ctx_size,)),
+            dma((2 * ctx_size,)),
+            dma((ctx_size,)),
+            dma((ctx_size,)),
+            dma((nv,)),
+            dma((nv,)),
+            dma,
+            dma((2 * devices,)),
+            dma((2 * devices,)),
+            dma((devices,)),
+            dma((devices,)),
+        ],
+        compiler_params=pltpu.CompilerParams(
+            collective_id=0, has_side_effects=True, vmem_limit_bytes=60 * 1024 * 1024
+        ),
+        name="window",
+    )(
+        block_query,
+        block_key,
+        block_value,
+        block_doc.reshape(1, blk),
+        token_query,
+        token_key,
+        token_value,
+        token_state,
+        norm_gain.reshape(1, width),
+        head_weight,
+        targets.reshape(tokens // 128, 128),
     )
-    block_context = (
-        (mixed / totals[..., None]).reshape(local_rows, head_count * HEAD_DIM).astype(jnp.bfloat16)
-    )
-    grouped = lax.all_to_all(block_context, "vocab", split_axis=0, concat_axis=1, tiled=True)
-    hidden = local_decoder(grouped, token_query, token_key, token_value, token_state, norm_gain)
-    return (block_context, head_priors(sizes, hidden, head_weight, targets))
+    return context, prior.reshape(tok)
 
 
 def solution(mesh):

time: 141 us -> 109 us (0.77)
  blocking collectives: 34.9 us -> 0 us
  Pallas kernels: 82.6 us -> 105 us
  starting transfers between devices: 4.88 us -> 0 us
  local copies, waits for them, and re-layouts: 7.39 us -> 2.73 us
  waiting for transfers between devices: 3.48 us -> 0 us
  other arithmetic: 3.4 us -> 0 us
  matrix products: 2.79 us -> 0 us
    pallas_call x1, Pallas kernels: 82.6 us -> 105 us  [local(): pl.pallas_call(functools.partial(kernel, sizes), out_shape=(jax.ShapeDtyp...]
    all_gather x2 -> x0, blocking collectives: 19.8 us -> none  [the longest x1 10 us: local(): values = lax.all_gather(block_value, 'ctx', axis=0, tiled=True)]
    unnamed x1 -> x0, blocking collectives: 15.1 us -> none
    all_to_all x1 -> x0, starting transfers between devices: 4.88 us -> none  [local(): lax.all_to_all(block_context, 'vocab', split_axis=0, concat_axis=1, tiled...]
    all_to_all x1 -> x0, waiting for transfers between devices: 3.48 us -> none  [local(): lax.all_to_all(block_context, 'vocab', split_axis=0, concat_axis=1, tiled...]
    dot_general x4 -> x0, matrix products: 2.79 us -> none  [the longest x1 1.24 us: local_decoder(): jnp.einsum('bhij,bjhd->bihd', weights.astype(jnp.bfloat16), values, prefe...]
    convert_element_type x2 -> x0, other arithmetic: 1.75 us -> none  [the longest x1 1.03 us: local_decoder(): return (summed * lax.rsqrt(power + 1e-05) * norm_gain).astype(jnp.bfloat16)]
  transfers between devices with their start and end apart: 1 -> 0, of which waited for: 1 -> 0; matrix products, arithmetic and copies ran while one was open for 2% -> 0% of each run, Pallas kernels for 0% -> 0%
where the time goes in v2:
time: 109 us
  Pallas kernels  105 us (96%)
  local copies, waits for them, and re-layouts  2.73 us (3%)
    pallas_call x1, Pallas kernels, local(): pl.pallas_call(functools.partial(kernel, sizes), out_shape=(jax.ShapeDtyp...  105 us
    unnamed x2, local copies, waits for them, and re-layouts  2.73 us

profile of v2, /device:TPU:0, one launch (start us, length us, event | category | flops | bytes accessed | tf_op | source)
XLA Modules:
  0.0 108.7 jit_solution(13503941251314426910)
XLA Ops:
  0.6 105.3 %window.1 = (bf16[32,1536]{1,0:T(8,128)(2,1)}, f32[1,32]{1,0:T(1,128)}) custom-call(bf16[32,1536]{1,0:T(8,128)(2,1)} %bq_hbm.1, bf16[32,1536]{1,0:T(8,128)(2,1)} %bk_hbm.1, bf16[32,1536]{1,0:T(8,128)(2,1)} %bv_hbm.1, s32[1,32]{1,0:T(1,128)} %bitcast.6, bf16[32,6144]{1,0:T(8,128)(2,1)} %tq_hbm.1, bf16[32,6144]{1,0:T(8,128)(2,1)} %tk_hbm.1, ...), custom_call_target="tpu_custom_call" | custom-call | tf_op jit(solution)/shard_map/window/pallas_call | solution.py:456
  106.0 1.5 %copy.15 = bf16[32,1536]{1,0:T(8,128)(2,1)} copy(bf16[32,1536]{1,0:T(8,128)(2,1)} %get-tuple-element.8) | data formatting | bytes 196608
  107.5 1.2 %copy.16 = f32[32]{0:T(128)} copy(f32[32]{0:T(128)} %bitcast.7) | data formatting | bytes 256

commit v3 on v2

--- a/solution.py
+++ b/solution.py
@@ -77,7 +77,10 @@
     nv, chips = place.nv, place.chips
     tok, width = ts.shape
     cols = w_ref.shape[1]
-    half_width = width // 2
+    units = width // 128
+    late = units * 5 // 48
+    early = units // 2 - late
+    widths = [early * 128, early * 128, late * 128, late * 128]
     per_group = nv * 2
     group = per_group * tok
     blk, part = bq.shape
@@ -275,99 +278,105 @@
 
     sent = []
 
-    def view(slot, half):
-        return rows.at[pl.ds(slot * tok, tok), pl.ds(half * half_width, half_width)]
-
-    def push(src, half, dst, device):
+    def view(slot, piece):
+        return rows.at[pl.ds(slot * tok, tok), pl.ds(sum(widths[:piece]), widths[piece])]
+
+    def push(src, piece, dst, device):
         dst_slot = place.slot(*dst)
         copy = pltpu.make_async_remote_copy(
-            src_ref=view(place.slot(*src), half),
-            dst_ref=view(dst_slot, half),
+            src_ref=view(place.slot(*src), piece),
+            dst_ref=view(dst_slot, piece),
             send_sem=send.at[len(sent)],
-            recv_sem=recv.at[2 * dst_slot + half],
+            recv_sem=recv.at[4 * dst_slot + piece],
             device_id=device,
             device_id_type=MESH,
         )
         copy.start()
         sent.append(copy)
 
-    def arrived(r, s, c, half):
+    def arrived(r, s, c, piece):
         slot = place.slot(r, s, c)
-        pltpu.make_async_copy(view(slot, half), view(slot, half), recv.at[2 * slot + half]).wait()
-
-    def along_vocab(s, half):
-        mid = nv // 2
-        ahead = s < mid - 1 or (s == mid - 1 and half == 0)
-        back = s == 0 or s > mid + 1 or (s == mid + 1 and half == 1)
+        ref = view(slot, piece)
+        pltpu.make_async_copy(ref, ref, recv.at[4 * slot + piece]).wait()
+
+    def along_vocab(r, s, piece):
+        mid, half = nv // 2, piece % 2
         if s == 0:
             ahead = mid > 1 or half == 0
             back = mid > 1 or half == 1
+        else:
+            ahead = s < mid - 1 or (s == mid - 1 and half == 0)
+            back = s > mid + 1 or (s == mid + 1 and half == 1)
         if ahead:
-            push((0, s, 0), half, (0, s + 1, 0), place.device(0, nv - 1, 0))
+            push((r, s, 0), piece, (r, s + 1, 0), place.device(0, nv - 1, 0))
         if back:
-            push((0, s, 0), half, (0, (s - 1) % nv, 0), place.device(0, 1, 0))
-
-    def pass_on(r, s, half):
-        if r == 0:
-            along_vocab(s, half)
-        for bit in place.onward(r, half):
-            push((r, s, 0), half, (r ^ bit, s, 0), place.device(bit, 0, 0))
-        push((r, s, 0), half, (r, s, 1), place.device(0, 0, 1))
+            push((r, s, 0), piece, (r, (s - 1) % nv, 0), place.device(0, 1, 0))
+
+    def along_ctx(r, s, piece):
+        for bit in place.onward(r, piece % 2):
+            push((r, s, 0), piece, (r ^ bit, s, 0), place.device(bit, 0, 0))
+
+    def take(r, s, piece):
+        arrived(r, s, 0, piece)
+        if r == 0 or piece > 1:
+            along_vocab(r, s, piece)
+        if s == 0 or piece < 2:
+            along_ctx(r, s, piece)
+        push((r, s, 0), piece, (r, s, 1), place.device(0, 0, 1))
 
     order = [0]
     for d in range(1, nv // 2):
         order += [d, nv - d]
     order.append(nv // 2)
 
-    def take(r, s):
-        for half in range(2):
-            if r or s:
-                arrived(r, s, 0, half)
-            pass_on(r, s, half)
-
-    for half in range(2):
-        along_vocab(0, half)
-    for half in range(2):
-        for bit in place.bits:
-            push((0, 0, 0), half, (bit, 0, 0), place.device(bit, 0, 0))
-    for half in range(2):
-        push((0, 0, 0), half, (0, 0, 1), place.device(0, 0, 1))
+    for piece in range(2):
+        along_vocab(0, 0, piece)
+    for piece in (2, 3, 0, 1):
+        along_ctx(0, 0, piece)
+    for piece in range(2, 4):
+        along_vocab(0, 0, piece)
+    for piece in range(4):
+        push((0, 0, 0), piece, (0, 0, 1), place.device(0, 0, 1))
 
     first = place.ctx * nv + place.z
     s_sent = []
-    lane = lax.broadcasted_iota(jnp.int32, (tok, 128), 1)
-    column = lax.broadcasted_iota(jnp.int32, (tok, cols), 1) + first * cols
+    lane = lax.broadcasted_iota(jnp.int32, (128, 128), 1)
+    column = lax.broadcasted_iota(jnp.int32, (128, cols), 1) + first * cols
     column = column.astype(jnp.float32)
     tile = min(256, cols)
 
-    def compute(r):
+    span_rows = max(128, tok)
+    in_span = span_rows // tok
+
+    def ready(r):
         for s in range(nv):
-            for half in range(2):
-                arrived(r, s, 1, half)
-        base = r * group
-
+            for piece in range(4):
+                arrived(r, s, 1, piece)
+
+    def multiply(r):
         @pl.loop(0, cols // tile)
         def _(n):
             at = pl.ds(pl.multiple_of(n * tile, tile), tile)
             logits[:, at] = jnp.dot(
-                rows[pl.ds(base, group), :], w_ref[:, at], preferred_element_type=jnp.float32
+                rows[pl.ds(r * group, group), :], w_ref[:, at], preferred_element_type=jnp.float32
             )
 
-        @pl.loop(0, per_group)
-        def _(i):
-            at = pl.multiple_of(i * tok, tok)
-            block = logits[pl.ds(at, tok), :]
+    def reduce(r):
+        @pl.loop(0, group // span_rows)
+        def _(j):
+            at = pl.multiple_of(j * span_rows, span_rows)
+            block = logits[pl.ds(at, span_rows), :]
             top = jnp.max(block, axis=1, keepdims=True)
             mass = jnp.sum(jnp.exp(block - top), axis=1, keepdims=True)
-            wanted = t_col[pl.ds(pl.multiple_of(base + at, tok), tok), :]
+            wanted = t_col[pl.ds(r * group + at, span_rows), :]
             pick = jnp.sum(jnp.where(column == wanted, block, 0.0), axis=1, keepdims=True)
             packed = jnp.where(lane == 0, top, jnp.where(lane == 1, mass, pick))
-            if tok < 128:
-                packed = jnp.concatenate(
-                    [packed, jnp.zeros((128 - tok, 128), jnp.float32)], axis=0
-                )
-            s_out[r * per_group + i] = jnp.transpose(packed)[0:8, :]
-
+            turned = jnp.transpose(packed)[0:8, :]
+            for k in range(in_span):
+                shifted = turned if k == 0 else pltpu.roll(turned, 128 - k * tok, 1)
+                s_out[r * per_group + j * in_span + k] = shifted
+
+    def share_stats(r):
         for s in range(nv):
             for c in range(2):
                 slot, there = place.slot(r, s, c), place.slot(r, (nv - s) % nv, c)
@@ -389,28 +398,37 @@
     outer.sort(key=lambda r: (bin(r).count("1"), r))
     near = [r for r in outer if r in place.bits]
     far = [r for r in outer if r not in place.bits]
-    for r in near:
-        take(r, 0)
-    for s in order[1:]:
-        take(0, s)
-    for r in far:
-        take(r, 0)
-    for r in near:
-        for s in order[1:-1]:
-            take(r, s)
+    def pieces(r):
+        steps = [functools.partial(multiply, r), functools.partial(reduce, r)]
+        return steps + [functools.partial(share_stats, r)]
+
+    def takes(rs, ss):
+        return [(r, s, p) for r in rs for s in ss for p in (2, 3, 0, 1)]
+
+    mids, last = order[1:-1], order[-1:]
+    for event in takes(near, [0]) + takes([0], mids) + takes(far, [0]) + takes([0], last):
+        take(*event)
+    for event in takes(near, mids):
+        take(*event)
     load_w.wait()
-    compute(0)
-    for r in near:
-        take(r, order[-1])
-    for r in far:
-        for s in order[1:-1]:
-            take(r, s)
-    for r in near:
-        compute(r)
-    for r in far:
-        take(r, order[-1])
-    for r in far:
-        compute(r)
+    ready(0)
+    pending = pieces(0)
+    for event in takes(near, last) + takes(far, mids):
+        take(*event)
+        if pending:
+            pending.pop(0)()
+    for step in pending:
+        step()
+    for r in near[:-1]:
+        ready(r)
+        for step in pieces(r):
+            step()
+    for event in takes(far, last):
+        take(*event)
+    for r in near[-1:] + far:
+        ready(r)
+        for step in pieces(r):
+            step()
 
     for copy in s_sent:
         copy.wait_recv()
@@ -487,8 +505,8 @@
             dma((nv,)),
             dma((nv,)),
             dma,
-            dma((2 * devices,)),
-            dma((2 * devices,)),
+            dma((4 * devices,)),
+            dma((4 * devices,)),
             dma((devices,)),
             dma((devices,)),
         ],

time: 109 us -> 103 us (0.945)
  Pallas kernels: 105 us -> 99.6 us
    pallas_call x1, Pallas kernels: 105 us -> 99.6 us  [local(): pl.pallas_call(functools.partial(kernel, sizes), out_shape=(jax.ShapeDtyp...]
where the time goes in v3:
time: 103 us
  Pallas kernels  99.6 us (97%)
  local copies, waits for them, and re-layouts  2.73 us (3%)
    pallas_call x1, Pallas kernels, local(): pl.pallas_call(functools.partial(kernel, sizes), out_shape=(jax.ShapeDtyp...  99.6 us
    unnamed x2, local copies, waits for them, and re-layouts  2.73 us

profile of v3, /device:TPU:0, one launch (start us, length us, event | category | flops | bytes accessed | tf_op | source)
XLA Modules:
  0.0 103.0 jit_solution(1616852539745230829)
XLA Ops:
  0.6 99.6 %window.1 = (bf16[32,1536]{1,0:T(8,128)(2,1)}, f32[1,32]{1,0:T(1,128)}) custom-call(bf16[32,1536]{1,0:T(8,128)(2,1)} %bq_hbm.1, bf16[32,1536]{1,0:T(8,128)(2,1)} %bk_hbm.1, bf16[32,1536]{1,0:T(8,128)(2,1)} %bv_hbm.1, s32[1,32]{1,0:T(1,128)} %bitcast.6, bf16[32,6144]{1,0:T(8,128)(2,1)} %tq_hbm.1, bf16[32,6144]{1,0:T(8,128)(2,1)} %tk_hbm.1, ...), custom_call_target="tpu_custom_call" | custom-call | tf_op jit(solution)/shard_map/window/pallas_call | solution.py:474
  100.3 1.5 %copy.15 = bf16[32,1536]{1,0:T(8,128)(2,1)} copy(bf16[32,1536]{1,0:T(8,128)(2,1)} %get-tuple-element.8) | data formatting | bytes 196608
  101.8 1.2 %copy.16 = f32[32]{0:T(128)} copy(f32[32]{0:T(128)} %bitcast.7) | data formatting | bytes 256
